TPU v7x, 512 devices: a whole 4x4x16 slice. The times are simulated.
512 devices in a mesh: dp: 16 (over y, x_hi, core), ctx: 32 (over z, x_lo).
Axes of the slice: x: 4 (x_hi: 2, x_lo: 2; x = x_hi * 2 + x_lo), y: 4, z: 16, core: 2. Of those that a mesh axis runs over, the one named last changes fastest.
Arguments:
- out_gate: bfloat16 [16, 8192, 512], P('dp', 'ctx'), may hold values from -6 to 6
- key_gate: bfloat16 [16, 8192, 512], P('dp', 'ctx'), may hold values from -6 to 6
- value_input: bfloat16 [16, 8192, 512], P('dp', 'ctx'), may hold values from -6 to 6
- filter_taps: bfloat16 [8192, 512], P('ctx'), may hold values from -2 to 2
- cotangent: bfloat16 [16, 8192, 512], P('dp', 'ctx'), may hold values from -6 to 6
- block_live: int32 [16, 128], P('dp', 'ctx'), may hold values 0 or 1
Outputs:
- grad_out_gate: bfloat16 [16, 8192, 512], P('dp', 'ctx')
- grad_key_gate: bfloat16 [16, 8192, 512], P('dp', 'ctx')
- grad_value: bfloat16 [16, 8192, 512], P('dp', 'ctx')
- grad_taps: bfloat16 [8192, 512], P('ctx')
Inputs may be any that keep to these rules, and one draw needn't show every extreme that they name: `block_live`: 1 where a block of 64 tokens holds sequence data, 0 where it is padding.
All inputs are finite; a program needn't handle non-finite values.
Results may differ from a plain program's by a relative error of at most 0.027.
Values may be sent and summed in bfloat16 or wider, within the bound.
A program may use at most 64 MiB of HBM per device.

v0:
```python
import math

import jax
import jax.numpy as jnp
from jax import lax
from jax.sharding import PartitionSpec as P

QLEN = 64
PROWS = 4


TWO_PI = 2.0 * math.pi


def angle_table(row_count, col_count, row_start, col_start, period_len, direction):
    row_ids = jnp.arange(row_count, dtype=jnp.int32)[:, None] + row_start
    col_ids = jnp.arange(col_count, dtype=jnp.int32)[None, :] + col_start
    phases = (row_ids * col_ids % period_len).astype(jnp.float32)
    return direction * TWO_PI * phases / period_len


def factor_tables(angles):
    return (jnp.cos(angles).astype(jnp.bfloat16), jnp.sin(angles).astype(jnp.bfloat16))


def rotate_pair(real_part, imag_part, angles):
    turn_cos = jnp.cos(angles)[None, :, :, None]
    turn_sin = jnp.sin(angles)[None, :, :, None]
    return (
        real_part * turn_cos - imag_part * turn_sin,
        real_part * turn_sin + imag_part * turn_cos,
    )


def forward_transform(signals):
    ctx_count = lax.axis_size("ctx")
    ctx_place = lax.axis_index("ctx")
    full_rows = 2 * signals.shape[1] * ctx_count
    col_count = signals.shape[2]
    col_share = col_count // ctx_count
    total_len = full_rows * col_count
    cos_rows, sin_rows = factor_tables(
        angle_table(full_rows, full_rows // 2, 0, 0, full_rows, -1.0)
    )
    twist_angles = angle_table(full_rows, col_share, 0, ctx_place * col_share, total_len, -1.0)
    cos_cols, sin_cols = factor_tables(angle_table(col_count, col_count, 0, 0, col_count, -1.0))
    spread = lax.all_to_all(signals, "ctx", split_axis=2, concat_axis=1, tiled=True)
    real_part = jnp.einsum("kp,spac->skac", cos_rows, spread, preferred_element_type=jnp.float32)
    imag_part = jnp.einsum("kp,spac->skac", sin_rows, spread, preferred_element_type=jnp.float32)
    real_part, imag_part = rotate_pair(real_part, imag_part, twist_angles)
    packed = jnp.stack([real_part, imag_part]).astype(jnp.bfloat16)
    regrouped = lax.all_to_all(packed, "ctx", split_axis=2, concat_axis=3, tiled=True)
    real_in = regrouped[0]
    imag_in = regrouped[1]
    real_out = jnp.einsum(
        "saqc,qk->sakc", real_in, cos_cols, preferred_element_type=jnp.float32
    ) - jnp.einsum("saqc,qk->sakc", imag_in, sin_cols, preferred_element_type=jnp.float32)
    imag_out = jnp.einsum(
        "saqc,qk->sakc", real_in, sin_cols, preferred_element_type=jnp.float32
    ) + jnp.einsum("saqc,qk->sakc", imag_in, cos_cols, preferred_element_type=jnp.float32)
    return jnp.stack([real_out, imag_out]).astype(jnp.bfloat16)


def inverse_transform(spectra):
    ctx_count = lax.axis_size("ctx")
    ctx_place = lax.axis_index("ctx")
    row_share = spectra.shape[2]
    col_count = spectra.shape[3]
    full_rows = row_share * ctx_count
    total_len = full_rows * col_count
    cos_cols, sin_cols = factor_tables(angle_table(col_count, col_count, 0, 0, col_count, 1.0))
    twist_angles = angle_table(row_share, col_count, ctx_place * row_share, 0, total_len, 1.0)
    cos_back, sin_back = factor_tables(angle_table(full_rows // 2, full_rows, 0, 0, full_rows, 1.0))
    real_in = spectra[0]
    imag_in = spectra[1]
    real_part = jnp.einsum(
        "sakc,kq->saqc", real_in, cos_cols, preferred_element_type=jnp.float32
    ) - jnp.einsum("sakc,kq->saqc", imag_in, sin_cols, preferred_element_type=jnp.float32)
    imag_part = jnp.einsum(
        "sakc,kq->saqc", real_in, sin_cols, preferred_element_type=jnp.float32
    ) + jnp.einsum("sakc,kq->saqc", imag_in, cos_cols, preferred_element_type=jnp.float32)
    real_part, imag_part = rotate_pair(real_part, imag_part, twist_angles)
    twisted = jnp.stack([real_part, imag_part]).astype(jnp.bfloat16)
    gathered = lax.all_to_all(twisted, "ctx", split_axis=3, concat_axis=2, tiled=True)
    signal = jnp.einsum(
        "pk,skac->spac", cos_back, gathered[0], preferred_element_type=jnp.float32
    ) - jnp.einsum("pk,skac->spac", sin_back, gathered[1], preferred_element_type=jnp.float32)
    spread = (signal * (1.0 / total_len)).astype(jnp.bfloat16)
    return lax.all_to_all(spread, "ctx", split_axis=1, concat_axis=2, tiled=True)


def spectrum_product(left_spec, right_spec, conjugate):
    left_real = left_spec[0].astype(jnp.float32)
    left_imag = left_spec[1].astype(jnp.float32)
    right_real = right_spec[0].astype(jnp.float32)
    right_imag = right_spec[1].astype(jnp.float32)
    if conjugate:
        real_out = left_real * right_real + left_imag * right_imag
        imag_out = left_imag * right_real - left_real * right_imag
    else:
        real_out = left_real * right_real - left_imag * right_imag
        imag_out = left_real * right_imag + left_imag * right_real
    return jnp.stack([real_out, imag_out]).astype(jnp.bfloat16)


def local(out_gate, key_gate, value_input, filter_taps, cotangent, block_live):
    tok_count = key_gate.shape[1]
    chan_count = key_gate.shape[2]
    block_count = block_live.shape[1]
    grid_shape = (PROWS, QLEN, chan_count)
    live_rows = block_live[0].astype(jnp.float32)[:, None, None]

    def masked(values):
        return (
            values.reshape(block_count, tok_count // block_count, chan_count) * live_rows
        ).reshape(tok_count, chan_count)

    key_wide = key_gate[0].astype(jnp.float32)
    value_wide = value_input[0].astype(jnp.float32)
    cot_wide = cotangent[0].astype(jnp.float32)
    gated_input = masked(key_wide * value_wide).astype(jnp.bfloat16).reshape(grid_shape)
    back_signal = (
        (cot_wide * out_gate[0].astype(jnp.float32)).astype(jnp.bfloat16).reshape(grid_shape)
    )
    taps_grid = filter_taps.reshape(grid_shape)
    filter_spec = None
    extra_signals = [taps_grid]
    first_spectra = forward_transform(jnp.stack([gated_input] + extra_signals))
    filter_spec = first_spectra[:, 1]
    forward_spec = first_spectra[:, 0]
    conv_out = inverse_transform(spectrum_product(forward_spec, filter_spec, False)[:, None])[0]
    backward_spec = forward_transform(back_signal[None])[:, 0]
    restored = inverse_transform(
        jnp.stack(
            [
                spectrum_product(backward_spec, filter_spec, True),
                spectrum_product(backward_spec, forward_spec, True),
            ],
            axis=1,
        )
    )
    grad_conv = restored[0]
    taps_seq = restored[1]
    conv_flat = conv_out.reshape(tok_count, chan_count).astype(jnp.float32)
    grad_gate = (cot_wide * conv_flat).astype(jnp.bfloat16)
    grad_flat = grad_conv.reshape(tok_count, chan_count).astype(jnp.float32)
    grad_key = masked(grad_flat * value_wide).astype(jnp.bfloat16)
    grad_value = masked(grad_flat * key_wide).astype(jnp.bfloat16)
    scale_factor = 1.0 / math.sqrt(lax.axis_size("dp") * tok_count * lax.axis_size("ctx"))
    taps_sum = lax.psum(
        taps_seq.reshape(tok_count, chan_count).astype(jnp.float32).astype(jnp.bfloat16), "dp"
    ).astype(jnp.float32)
    grad_taps = (taps_sum * scale_factor).astype(jnp.bfloat16)
    return (grad_gate[None], grad_key[None], grad_value[None], grad_taps)


def solution(mesh):
    return jax.shard_map(
        local,
        mesh=mesh,
        in_specs=(
            P("dp", "ctx", None),
            P("dp", "ctx", None),
            P("dp", "ctx", None),
            P("ctx", None),
            P("dp", "ctx", None),
            P("dp", "ctx"),
        ),
        out_specs=(
            P("dp", "ctx", None),
            P("dp", "ctx", None),
            P("dp", "ctx", None),
            P("ctx", None),
        ),
        check_vma=False,
    )
```

profile of v0, /device:TPU:1, one launch (start us, length us, event | category | flops | bytes accessed | tf_op | source)
XLA Modules:
  0.0 641.4 jit_solution(15273747222807358933)
XLA Ops:
  7.2 1.6 fusion.64
  8.9 0.9 copy.209
  9.8 17.0 %all-to-all-start.4 = ((bf16[1,4,64,512]{3,1,0,2:T(4,128)(2,1)}), bf16[1,4,64,512]{3,1,0,2:T(4,128)(2,1)S(1)}, u32[]{:S(2)}, u32[]{:S(2)}) async-start(bf16[1,4,64,512]{3,1,0,2:T(4,128)(2,1)} %copy.209), calls=%async_computation.4 | async-start | bytes 524288 | tf_op jit(solution)/shard_map/all_to_all | solution.py:47
  26.8 0.5 fusion.67
  27.6 1.2 copy.191
  28.8 18.5 %all-to-all-done.4 = bf16[1,4,64,512]{3,1,0,2:T(4,128)(2,1)S(1)} async-done(((bf16[1,4,64,512]{3,1,0,2:T(4,128)(2,1)}), bf16[1,4,64,512]{3,1,0,2:T(4,128)(2,1)S(1)}, u32[]{:S(2)}, u32[]{:S(2)}) %all-to-all-start.4) | async-done | bytes 262176 | tf_op jit(solution)/shard_map/all_to_all | solution.py:47
  47.3 3.9 all-to-all-start
  51.8 0.8 convolution_bitcast_fusion
  52.6 0.9 fusion.51
  53.6 2.1 copy.213
  55.7 26.1 %all-to-all-done = bf16[2,4,64,512]{3,1,0,2:T(4,128)(2,1)S(1)} async-done(((bf16[2,4,64,512]{3,1,0,2:T(4,128)(2,1)}), bf16[2,4,64,512]{3,1,0,2:T(4,128)(2,1)S(1)}, u32[]{:S(2)}, u32[]{:S(2)}) %all-to-all-start) | async-done | bytes 524320 | tf_op jit(solution)/shard_map/all_to_all | solution.py:47
  81.8 4.6 all-to-all-start.5
  87.3 0.9 fusion.82
  88.2 1.1 fusion.39
  89.6 4.1 copy.196
  93.7 44.4 %all-to-all-done.5 = bf16[2,1,256,2,512]{4,3,1,0,2:T(2,128)(2,1)S(1)} async-done(((bf16[2,1,256,2,512]{4,3,1,0,2:T(2,128)(2,1)}), bf16[2,1,256,2,512]{4,3,1,0,2:T(2,128)(2,1)S(1)}, u32[]{:S(2)}, u32[]{:S(2)}) %all-to-all-start.5) | async-done | bytes 1048608 | tf_op jit(solution)/shard_map/all_to_all | solution.py:52
  138.1 6.8 %all-to-all-start.1 = ((bf16[2,2,256,2,512]{4,3,1,0,2:T(2,128)(2,1)}), bf16[2,2,256,2,512]{4,3,1,0,2:T(2,128)(2,1)S(1)}, u32[]{:S(2)}, u32[]{:S(2)}) async-start(bf16[2,2,256,2,512]{4,3,1,0,2:T(2,128)(2,1)} %copy.196), calls=%async_computation.1 | async-start | bytes 4194304 | tf_op jit(solution)/shard_map/all_to_all | solution.py:52
  145.2 0.9 fusion.228
  146.1 0.5 copy.215
  146.9 2.4 copy.216
  149.2 1.2 reshape.608
  150.9 1.4 fusion.18
  152.3 1.4 fusion.103
  153.7 86.9 %all-to-all-done.1 = bf16[2,2,256,2,512]{4,3,1,0,2:T(2,128)(2,1)S(1)} async-done(((bf16[2,2,256,2,512]{4,3,1,0,2:T(2,128)(2,1)}), bf16[2,2,256,2,512]{4,3,1,0,2:T(2,128)(2,1)S(1)}, u32[]{:S(2)}, u32[]{:S(2)}) %all-to-all-start.1) | async-done | bytes 2097184 | tf_op jit(solution)/shard_map/all_to_all | solution.py:52
  240.6 0.7 copy.287
  241.3 1.2 fusion.227
  242.5 1.1 copy.198
  244.0 1.9 fusion.111
  246.4 0.7 copy-done
  247.1 2.1 copy.199
  249.2 1.5 squeeze.13
  250.7 2.1 fusion.9
  252.8 0.5 fusion.8
  254.5 1.1 fusion.33
  256.8 0.6 fusion.49
  257.5 1.6 copy.200
  259.0 7.4 %all-to-all-start.2 = ((bf16[2,1,8,64,512]{4,2,1,0,3:T(8,128)(2,1)}), bf16[2,1,8,64,512]{4,2,1,0,3:T(8,128)(2,1)S(1)}, u32[]{:S(2)}, u32[]{:S(2)}) async-start(bf16[2,1,8,64,512]{4,2,1,0,3:T(8,128)(2,1)} %copy.200), calls=%async_computation.2 | async-start | bytes 2097152 | tf_op jit(solution)/shard_map/all_to_all | solution.py:84
  267.2 0.5 fusion.48
  267.7 0.5 convolution_add_fusion
  268.3 0.9 fusion.41
  269.4 2.5 copy.217
  271.9 47.3 %all-to-all-done.2 = bf16[2,1,8,64,512]{4,2,1,0,3:T(8,128)(2,1)S(1)} async-done(((bf16[2,1,8,64,512]{4,2,1,0,3:T(8,128)(2,1)}), bf16[2,1,8,64,512]{4,2,1,0,3:T(8,128)(2,1)S(1)}, u32[]{:S(2)}, u32[]{:S(2)}) %all-to-all-start.2) | async-done | bytes 1048608 | tf_op jit(solution)/shard_map/all_to_all | solution.py:84
  319.2 5.9 all-to-all-start.6
  325.3 0.8 fusion.61
  326.0 0.8 fusion.25
  326.9 0.9 copy.206
  327.7 93.3 %all-to-all-done.6 = bf16[2,2,8,64,512]{4,2,1,0,3:T(8,128)(2,1)S(1)} async-done(((bf16[2,2,8,64,512]{4,2,1,0,3:T(8,128)(2,1)}), bf16[2,2,8,64,512]{4,2,1,0,3:T(8,128)(2,1)S(1)}, u32[]{:S(2)}, u32[]{:S(2)}) %all-to-all-start.6) | async-done | bytes 2097184 | tf_op jit(solution)/shard_map/all_to_all | solution.py:84
  421.0 7.3 %all-to-all-start.3 = ((bf16[1,128,2,512]{3,2,0,1:T(2,128)(2,1)}), bf16[1,128,2,512]{3,2,0,1:T(2,128)(2,1)S(1)}, u32[]{:S(2)}, u32[]{:S(2)}) async-start(bf16[1,128,2,512]{3,2,0,1:T(2,128)(2,1)} %copy.206), calls=%async_computation.3 | async-start | bytes 524288 | tf_op jit(solution)/shard_map/all_to_all | solution.py:89
  428.8 0.9 fusion.43
  429.7 1.0 fusion.22
  430.7 1.1 copy.223
  431.8 16.0 %all-to-all-done.3 = bf16[1,128,2,512]{3,2,0,1:T(2,128)(2,1)S(1)} async-done(((bf16[1,128,2,512]{3,2,0,1:T(2,128)(2,1)}), bf16[1,128,2,512]{3,2,0,1:T(2,128)(2,1)S(1)}, u32[]{:S(2)}, u32[]{:S(2)}) %all-to-all-start.3) | async-done | bytes 262176 | tf_op jit(solution)/shard_map/all_to_all | solution.py:89
  447.8 4.8 all-to-all-start.7
  453.4 0.5 copy.207
  453.9 0.6 fusion.59
  454.5 0.7 copy.228
  455.3 26.7 %all-to-all-done.7 = bf16[2,128,2,512]{3,2,0,1:T(2,128)(2,1)S(1)} async-done(((bf16[2,128,2,512]{3,2,0,1:T(2,128)(2,1)}), bf16[2,128,2,512]{3,2,0,1:T(2,128)(2,1)S(1)}, u32[]{:S(2)}, u32[]{:S(2)}) %all-to-all-start.7) | async-done | bytes 524320 | tf_op jit(solution)/shard_map/all_to_all | solution.py:89
  482.4 0.5 copy.226
  483.2 0.8 reshape_squeeze.2
  484.0 2.6 fusion.58
  486.7 0.7 copy.229
  487.4 0.7 copy.230
  488.1 144.7 %all-reduce.2.cloned.1.call-done = bf16[256,512]{1,0:T(8,128)(2,1)} async-done(((bf16[256,512]{1,0:T(8,128)(2,1)}), bf16[256,512]{1,0:T(8,128)(2,1)}) %all-reduce.2.cloned.1.call-update) | async-done | bytes 262160 | tf_op jit(solution)/shard_map/psum | solution.py:150
  632.9 1.7 multiply_convert_fusion
  (60 shorter events, 9.2 us)
Async XLA Ops:
  7.2 19.6 %copy-start.6 = (bf16[1,256,512]{2,1,0:T(8,128)(2,1)S(1)}, bf16[1,256,512]{2,1,0:T(8,128)(2,1)}, u32[]{:S(2)}) copy-start(bf16[1,256,512]{2,1,0:T(8,128)(2,1)} %param.7) | copy-start | bytes 786436
  7.2 19.6 %copy-start.7 = (bf16[1,256,512]{2,1,0:T(8,128)(2,1)S(1)}, bf16[1,256,512]{2,1,0:T(8,128)(2,1)}, u32[]{:S(2)}) copy-start(bf16[1,256,512]{2,1,0:T(8,128)(2,1)} %param.8) | copy-start | bytes 786436
  8.8 18.6 %copy-start.10 = (s32[1,4]{1,0:T(1,128)S(1)}, s32[1,4]{1,0:T(1,128)}, u32[]{:S(2)}) copy-start(s32[1,4]{1,0:T(1,128)} %param.11) | copy-start | bytes 52
  8.9 18.6 %copy-start.9 = (bf16[256,512]{1,0:T(8,128)(2,1)S(1)}, bf16[256,512]{1,0:T(8,128)(2,1)}, u32[]{:S(2)}) copy-start(bf16[256,512]{1,0:T(8,128)(2,1)} %param.9) | copy-start | bytes 786436
  9.8 37.5 %all-to-all-start.4 = ((bf16[1,4,64,512]{3,1,0,2:T(4,128)(2,1)}), bf16[1,4,64,512]{3,1,0,2:T(4,128)(2,1)S(1)}, u32[]{:S(2)}, u32[]{:S(2)}) async-start(bf16[1,4,64,512]{3,1,0,2:T(4,128)(2,1)} %copy.209), calls=%async_computation.4 | async-start | bytes 524288 | tf_op jit(solution)/shard_map/all_to_all | solution.py:47
  47.3 34.5 %all-to-all-start = ((bf16[2,4,64,512]{3,1,0,2:T(4,128)(2,1)}), bf16[2,4,64,512]{3,1,0,2:T(4,128)(2,1)S(1)}, u32[]{:S(2)}, u32[]{:S(2)}) async-start(bf16[2,4,64,512]{3,1,0,2:T(4,128)(2,1)} %copy.191), calls=%async_computation | async-start | bytes 1048576 | tf_op jit(solution)/shard_map/all_to_all | solution.py:47
  81.8 56.3 %all-to-all-start.5 = ((bf16[2,1,256,2,512]{4,3,1,0,2:T(2,128)(2,1)}), bf16[2,1,256,2,512]{4,3,1,0,2:T(2,128)(2,1)S(1)}, u32[]{:S(2)}, u32[]{:S(2)}) async-start(bf16[2,1,256,2,512]{4,3,1,0,2:T(2,128)(2,1)} %copy.213), calls=%async_computation.5 | async-start | bytes 2097152 | tf_op jit(solution)/shard_map/all_to_all | solution.py:52
  138.1 102.5 %all-to-all-start.1 = ((bf16[2,2,256,2,512]{4,3,1,0,2:T(2,128)(2,1)}), bf16[2,2,256,2,512]{4,3,1,0,2:T(2,128)(2,1)S(1)}, u32[]{:S(2)}, u32[]{:S(2)}) async-start(bf16[2,2,256,2,512]{4,3,1,0,2:T(2,128)(2,1)} %copy.196), calls=%async_computation.1 | async-start | bytes 4194304 | tf_op jit(solution)/shard_map/all_to_all | solution.py:52
  150.5 1.8 copy-start.1
  245.9 1.2 copy-start
  252.8 1.0 copy-start.2
  252.8 1.4 copy-start.3
  252.8 1.7 copy-start.4
  259.0 60.2 %all-to-all-start.2 = ((bf16[2,1,8,64,512]{4,2,1,0,3:T(8,128)(2,1)}), bf16[2,1,8,64,512]{4,2,1,0,3:T(8,128)(2,1)S(1)}, u32[]{:S(2)}, u32[]{:S(2)}) async-start(bf16[2,1,8,64,512]{4,2,1,0,3:T(8,128)(2,1)} %copy.200), calls=%async_computation.2 | async-start | bytes 2097152 | tf_op jit(solution)/shard_map/all_to_all | solution.py:84
  319.2 101.8 %all-to-all-start.6 = ((bf16[2,2,8,64,512]{4,2,1,0,3:T(8,128)(2,1)}), bf16[2,2,8,64,512]{4,2,1,0,3:T(8,128)(2,1)S(1)}, u32[]{:S(2)}, u32[]{:S(2)}) async-start(bf16[2,2,8,64,512]{4,2,1,0,3:T(8,128)(2,1)} %copy.217), calls=%async_computation.6 | async-start | bytes 4194304 | tf_op jit(solution)/shard_map/all_to_all | solution.py:84
  421.0 26.8 %all-to-all-start.3 = ((bf16[1,128,2,512]{3,2,0,1:T(2,128)(2,1)}), bf16[1,128,2,512]{3,2,0,1:T(2,128)(2,1)S(1)}, u32[]{:S(2)}, u32[]{:S(2)}) async-start(bf16[1,128,2,512]{3,2,0,1:T(2,128)(2,1)} %copy.206), calls=%async_computation.3 | async-start | bytes 524288 | tf_op jit(solution)/shard_map/all_to_all | solution.py:89
  430.7 23.3 %copy-start.5 = (bf16[1,256,512]{2,1,0:T(8,128)(2,1)S(1)}, bf16[1,256,512]{2,1,0:T(8,128)(2,1)}, u32[]{:S(2)}) copy-start(bf16[1,256,512]{2,1,0:T(8,128)(2,1)} %param.10) | copy-start | bytes 786436
  447.8 34.2 %all-to-all-start.7 = ((bf16[2,128,2,512]{3,2,0,1:T(2,128)(2,1)}), bf16[2,128,2,512]{3,2,0,1:T(2,128)(2,1)S(1)}, u32[]{:S(2)}, u32[]{:S(2)}) async-start(bf16[2,128,2,512]{3,2,0,1:T(2,128)(2,1)} %copy.223), calls=%async_computation.7 | async-start | bytes 1048576 | tf_op jit(solution)/shard_map/all_to_all | solution.py:89
  452.6 180.2 %all-reduce.2.cloned.1.call-start = ((), (), s32[]{:S(2)}) async-start(), calls=%async_computation.8 | async-start | bytes 524288 | tf_op jit(solution)/shard_map/psum | solution.py:150
  482.3 1.7 copy-start.8
Sparse Core Ops, SparseCore 0:
  484.1 148.6 all-reduce.1
where the time goes:
time: 642 us; the launch traced here: 641 us
  waiting for transfers between devices  504 us (79%)
  starting transfers between devices  58 us (9%)
  local copies, waits for them, and re-layouts  35.6 us (6%)
  matrix products  20.7 us (3%)
  between operations  14.6 us (2%)
  other arithmetic  8.59 us (1%)
    psum x1, waiting for transfers between devices, local(): lax.psum(taps_seq.reshape(tok_count, chan_count).astype(jnp.float32).asty...  145 us
    all_to_all x2, waiting for transfers between devices, inverse_transform(): lax.all_to_all(twisted, 'ctx', split_axis=3, concat_axis=2, tiled=True)  141 us
    all_to_all x2, waiting for transfers between devices, forward_transform(): lax.all_to_all(packed, 'ctx', split_axis=2, concat_axis=3, tiled=True)  131 us
    all_to_all x2, waiting for transfers between devices, forward_transform(): lax.all_to_all(signals, 'ctx', split_axis=2, concat_axis=1, tiled=True)  44.6 us
    all_to_all x2, waiting for transfers between devices, inverse_transform(): lax.all_to_all(spread, 'ctx', split_axis=1, concat_axis=2, tiled=True)  42.7 us
    all_to_all x2, starting transfers between devices, forward_transform(): lax.all_to_all(signals, 'ctx', split_axis=2, concat_axis=1, tiled=True)  20.9 us
    all_to_all x2, starting transfers between devices, inverse_transform(): lax.all_to_all(twisted, 'ctx', split_axis=3, concat_axis=2, tiled=True)  13.3 us
  transfers between devices with their start and end apart: 9, of which 9 were waited for; matrix products, arithmetic and copies ran while one was open for 6% of the time, Pallas kernels for 0%

commit v1 on v0

v1 whole, which is shorter than its diff:
```python
import functools
import math

import jax
import jax.numpy as jnp
import ml_dtypes
import numpy as np
from jax import lax
from jax.experimental import pallas as pl
from jax.experimental.pallas import tpu as pltpu
from jax.sharding import PartitionSpec as P

MESH = pl.DeviceIdType.MESH
F32 = jnp.float32
BF16 = jnp.bfloat16


@functools.lru_cache(maxsize=None)
def tables(parts, length, group):
    full = 2 * parts
    low = np.arange(parts + 1)
    block = np.arange(parts)
    step = np.arange(length)
    turn = 2.0 * np.pi / full * (low[:, None] * block[None, :] % full)
    eye = np.eye(group)
    spread = lambda m: np.kron(m, eye)
    cos1, sin1 = np.cos(turn), np.sin(turn)
    first = np.concatenate([spread(cos1), spread(-sin1[1:parts])], axis=0)
    weight = np.full((parts + 1, 1), 2.0)
    weight[0] = weight[parts] = 1.0
    last = np.concatenate([spread((weight * cos1).T), spread((-weight * sin1)[1:parts].T)], axis=1)
    cols = 2.0 * np.pi / length * (step[:, None] * step[None, :] % length)
    cos2, sin2 = np.cos(cols), np.sin(cols)
    fwd = np.block([[cos2, -sin2], [sin2, cos2]])
    inv = np.block([[cos2, sin2], [-sin2, cos2]])
    twist = 2.0 * np.pi / (full * length) * (low[:, None] * step[None, :])
    rows = lambda m: np.repeat(m[:, None, :], 8, axis=1).astype(np.float32)
    half = lambda m: m.astype(np.float32).astype(ml_dtypes.bfloat16)
    return (half(first), half(fwd), half(inv), half(last), rows(np.cos(twist)), rows(np.sin(twist)))


def kernel(
    devices,
    live,
    key_hbm,
    val_hbm,
    taps_hbm,
    cot_hbm,
    gate_hbm,
    first_hbm,
    fwd_hbm,
    inv_hbm,
    last_hbm,
    tcos_hbm,
    tsin_hbm,
    out_gate,
    out_key,
    out_val,
    out_taps,
    key,
    val,
    taps,
    cot,
    gate,
    first,
    fwd,
    inv,
    last,
    tcos,
    tsin,
    gated_s,
    back_s,
    filt_s,
    gated_r,
    back_r,
    filt_r,
    conv_s,
    grad_s,
    taps_s,
    conv_r,
    grad_r,
    sums_r,
    total,
    taps_r,
    spec_f,
    spec_b,
    spec_h,
    twisted,
    load_sem,
    send_sem,
    recv_sem,
    small_sem,
):
    n_dp, n_ctx = devices
    n_z = n_ctx // 2
    d = lax.axis_index("dp")
    c = lax.axis_index("ctx")
    z, x = c // 2, c % 2
    chans, length = n_ctx * gated_s.shape[1], gated_s.shape[2]
    group = gated_s.shape[1]
    n_low = n_ctx + 1
    blocks = live.shape[1]
    block = length // blocks

    def shift_of(place):
        pair, core = place // 2, place % 2
        return pair + core * (n_dp - 2 * pair - (n_dp // 2) * ((n_dp - pair) // n_dp))

    shift = shift_of(d)
    pair_in = (z + shift) % n_z
    pair_out = (z - shift + n_z) % n_z

    loads = [
        pltpu.make_async_copy(src, dst, load_sem.at[i])
        for i, (src, dst) in enumerate(
            [
                (taps_hbm, taps),
                (key_hbm, key),
                (val_hbm, val),
                (cot_hbm, cot),
                (gate_hbm, gate),
                (first_hbm, first),
                (tcos_hbm, tcos),
                (tsin_hbm, tsin),
                (fwd_hbm, fwd),
                (inv_hbm, inv),
                (last_hbm, last),
            ]
        )
    ]
    for load in loads:
        load.start()

    barrier = pltpu.get_barrier_semaphore()

    def greet_ctx(k, carry):
        pl.semaphore_signal(barrier, inc=1, device_id=(d, (c + k) % n_ctx), device_id_type=MESH)
        return carry

    def greet_dp(k, carry):
        pl.semaphore_signal(barrier, inc=1, device_id=((d + k) % n_dp, c), device_id_type=MESH)
        return carry

    lax.fori_loop(1, n_ctx, greet_ctx, 0)
    lax.fori_loop(1, n_dp, greet_dp, 0)

    def remote(src, dst, send, recv, to):
        return pltpu.make_async_remote_copy(
            src_ref=src, dst_ref=dst, send_sem=send, recv_sem=recv, device_id=to, device_id_type=MESH
        )

    def await_bytes(ref, sem):
        pltpu.make_async_copy(ref, ref, sem).wait()

    def exchange(src, dst, phase):
        def body(k, carry):
            zz = k // 2
            away = ((zz + 1) // 2) * (2 * (zz % 2) - 1)
            to = 2 * ((z + away + n_z) % n_z) + (x + k) % 2
            remote(src.at[to], dst.at[c], send_sem.at[phase], recv_sem.at[phase], (d, to)).start()
            return carry

        lax.fori_loop(1, n_ctx, body, 0)
        dst[c] = src[c]

    def exchanged(dst, phase):
        await_bytes(dst.at[pl.ds(0, n_ctx - 1)], recv_sem.at[phase])

    def exchange_sent(src, phase):
        await_bytes(src.at[pl.ds(0, n_ctx - 1)], send_sem.at[phase])

    def spread_dp(ref, place, phase):
        def body(k, carry):
            to = (d + k) % n_dp
            part = ref.at[pl.ds(place, 2)]
            remote(part, part, send_sem.at[phase], recv_sem.at[phase], (to, c)).start()
            return carry

        lax.fori_loop(1, n_dp, body, 0)

    def turned(values):
        return values.T.reshape(n_ctx, group, length)

    loads[0].wait()
    filt_s[...] = turned(taps[...])
    loads[1].wait()
    loads[2].wait()
    for b in range(blocks):
        rows = pl.ds(b * block, block)
        alive = live[0, b].astype(F32)
        key[0, rows] = key[0, rows] * alive.astype(BF16)
    gated_s[...] = turned((key[0].astype(F32) * val[0].astype(F32)).astype(BF16))

    pl.semaphore_wait(barrier, n_ctx - 1 + n_dp - 1)

    def filt_copy(side, to):
        return remote(filt_s.at[to], filt_r.at[c], small_sem.at[0, side], small_sem.at[1, side], (d, to))

    filt_other = filt_copy(1, 2 * pair_out + 1 - x)
    filt_same = filt_copy(0, 2 * pair_out + x)
    filt_other.start()

    @pl.when(shift != 0)
    def _():
        filt_same.start()

    @pl.when(shift == 0)
    def _():
        filt_r[c] = filt_s[c]

    exchange(gated_s, gated_r, 0)

    loads[3].wait()
    loads[4].wait()
    back_s[...] = turned((cot[0].astype(F32) * gate[0].astype(F32)).astype(BF16))
    exchange(back_s, back_r, 1)

    filt_other.wait_recv()

    @pl.when(shift != 0)
    def _():
        filt_same.wait_recv()

    spread_dp(filt_r, 2 * pair_in, 2)
    for load in loads[5:]:
        load.wait()

    low_groups = []
    per = -(-n_low // (3 if n_low % 3 == 0 else 2))
    for start in range(0, n_low, per):
        low_groups.append((start, min(start + per, n_low)))

    def rotate(real, imag, lo, hi, sign):
        shape = (hi - lo, group // 8, 8, length)
        cosv = tcos[lo:hi][:, None]
        sinv = tsin[lo:hi][:, None]
        real, imag = real.reshape(shape), imag.reshape(shape)
        if sign > 0:
            out = (real * cosv - imag * sinv, real * sinv + imag * cosv)
        else:
            out = (real * cosv + imag * sinv, imag * cosv - real * sinv)
        return tuple(part.reshape((hi - lo) * group, length) for part in out)

    real_rows = n_low * group

    def forward(src, spec):
        signal = src[...].reshape(chans, length)
        for lo, hi in low_groups:
            real = jnp.dot(first[lo * group : hi * group], signal, preferred_element_type=F32)
            ilo, ihi = max(lo, 1), min(hi, n_low - 1)
            at = real_rows + (ilo - 1) * group
            imag = jnp.dot(first[at : at + (ihi - ilo) * group], signal, preferred_element_type=F32)
            parts = [imag]
            if lo == 0:
                parts = [jnp.zeros((group, length), F32)] + parts
            if hi == n_low:
                parts = parts + [jnp.zeros((group, length), F32)]
            imag = jnp.concatenate(parts, axis=0) if len(parts) > 1 else imag
            real, imag = rotate(real, imag, lo, hi, -1)
            pair = jnp.concatenate([real.astype(BF16), imag.astype(BF16)], axis=1)
            spec[lo * group : hi * group] = jnp.dot(pair, fwd[...], preferred_element_type=F32)

    def restore(left, right, conjugate, dst, scale):
        for lo, hi in low_groups:
            rows = slice(lo * group, hi * group)
            lr, li = left[rows, :length], left[rows, length:]
            rr, ri = right[rows, :length], right[rows, length:]
            if conjugate:
                real, imag = lr * rr + li * ri, li * rr - lr * ri
            else:
                real, imag = lr * rr - li * ri, lr * ri + li * rr
            pair = jnp.concatenate([real.astype(BF16), imag.astype(BF16)], axis=1)
            both = jnp.dot(pair, inv[...], preferred_element_type=F32)
            real, imag = rotate(both[:, :length], both[:, length:], lo, hi, 1)
            twisted[rows] = real.astype(BF16)
            ilo, ihi = max(lo, 1), min(hi, n_low - 1)
            at = real_rows + (ilo - 1) * group
            twisted[at : at + (ihi - ilo) * group] = imag[(ilo - lo) * group : (ihi - lo) * group].astype(BF16)
        rows_half = chans // 2
        for part in range(2):
            rows = slice(part * rows_half, (part + 1) * rows_half)
            signal = jnp.dot(last[rows], twisted[...], preferred_element_type=F32)
            dst[part * n_z : (part + 1) * n_z] = (signal * scale).astype(BF16).reshape(n_z, group, length)

    inv_len = 1.0 / (2 * n_ctx * length)
    await_bytes(filt_r.at[pl.ds(0, 2 * (n_dp - 1))], recv_sem.at[2])
    forward(filt_r, spec_h)
    exchanged(gated_r, 0)
    forward(gated_r, spec_f)
    restore(spec_f, spec_h, False, conv_s, inv_len)
    exchange(conv_s, conv_r, 3)

    exchanged(back_r, 1)
    forward(back_r, spec_b)
    restore(spec_b, spec_f, True, taps_s, inv_len)

    def share(k, carry):
        to = (d + k) % n_dp
        at = 2 * ((z + shift_of(to)) % n_z)
        remote(taps_s.at[pl.ds(at, 2)], sums_r.at[d], send_sem.at[4], recv_sem.at[4], (to, c)).start()
        return carry

    lax.fori_loop(1, n_dp, share, 0)
    sums_r[d] = taps_s[pl.ds(2 * pair_in, 2)]

    restore(spec_b, spec_h, True, grad_s, inv_len)
    exchange(grad_s, grad_r, 5)

    await_bytes(sums_r.at[pl.ds(0, n_dp - 1)], recv_sem.at[4])
    taps_scale = 1.0 / math.sqrt(n_dp * n_ctx * length)
    summed = sums_r[0].astype(F32)
    for i in range(1, n_dp):
        summed = summed + sums_r[i].astype(F32)
    total[...] = (summed * taps_scale).astype(BF16)

    def taps_copy(side, at):
        return remote(total.at[at], taps_r.at[c], small_sem.at[2, side], small_sem.at[3, side], (d, 2 * pair_in + at))

    taps_other = taps_copy(1, 1 - x)
    taps_same = taps_copy(0, x)
    taps_other.start()

    @pl.when(shift != 0)
    def _():
        taps_same.start()

    @pl.when(shift == 0)
    def _():
        taps_r[c] = total[x]

    def tokens(ref):
        return ref[...].reshape(chans, length).T.astype(F32)

    exchanged(conv_r, 3)
    out_gate[0] = (cot[0].astype(F32) * tokens(conv_r)).astype(BF16)

    taps_other.wait_recv()

    @pl.when(shift != 0)
    def _():
        taps_same.wait_recv()

    spread_dp(taps_r, 2 * pair_out, 6)
    await_bytes(taps_r.at[pl.ds(0, 2 * (n_dp - 1))], recv_sem.at[6])
    out_taps[...] = taps_r[...].reshape(chans, length).T

    exchanged(grad_r, 5)
    grad = tokens(grad_r)
    for b in range(blocks):
        rows = slice(b * block, (b + 1) * block)
        alive = live[0, b].astype(F32)
        out_key[0, rows] = (grad[rows] * val[0, rows].astype(F32) * alive).astype(BF16)
        out_val[0, rows] = (grad[rows] * key[0, rows].astype(F32) * alive).astype(BF16)

    filt_other.wait_send()
    taps_other.wait_send()

    @pl.when(shift != 0)
    def _():
        filt_same.wait_send()
        taps_same.wait_send()

    for src, phase in ((gated_s, 0), (back_s, 1), (conv_s, 3), (grad_s, 5)):
        exchange_sent(src, phase)
    for ref, phase in ((filt_r, 2), (taps_s, 4), (taps_r, 6)):
        await_bytes(ref.at[pl.ds(0, 2 * (n_dp - 1))], send_sem.at[phase])


def local(out_gate, key_gate, value_input, filter_taps, cotangent, block_live):
    n_dp, n_ctx = lax.axis_size("dp"), lax.axis_size("ctx")
    length, chans = key_gate.shape[1:]
    group = chans // n_ctx
    consts = tables(n_ctx, length, group)
    any_spec = pl.BlockSpec(memory_space=pl.ANY)
    signal = (1, length, chans)
    chunks = pltpu.VMEM((n_ctx, group, length), BF16)
    rows = (n_ctx + 1) * group
    scratch = (
        [pltpu.VMEM(signal, BF16)] * 2
        + [pltpu.VMEM(signal[1:], BF16)]
        + [pltpu.VMEM(signal, BF16)] * 2
        + [pltpu.VMEM(t.shape, F32 if t.dtype == np.float32 else BF16) for t in consts]
        + [chunks] * 11
        + [pltpu.VMEM((n_dp, 2, group, length), BF16), pltpu.VMEM((2, group, length), BF16), chunks]
        + [pltpu.VMEM((rows, 2 * length), F32)] * 3
        + [pltpu.VMEM((2 * n_ctx * group, length), BF16)]
        + [
            pltpu.SemaphoreType.DMA((11,)),
            pltpu.SemaphoreType.DMA((7,)),
            pltpu.SemaphoreType.DMA((7,)),
            pltpu.SemaphoreType.DMA((4, 2)),
        ]
    )
    vmem_spec = pl.BlockSpec(memory_space=pltpu.VMEM)
    call = pl.pallas_call(
        functools.partial(kernel, (n_dp, n_ctx)),
        out_shape=[jax.ShapeDtypeStruct(signal, BF16)] * 3 + [jax.ShapeDtypeStruct(signal[1:], BF16)],
        in_specs=[pl.BlockSpec(memory_space=pltpu.SMEM)] + [any_spec] * 11,
        out_specs=[vmem_spec] * 4,
        scratch_shapes=scratch,
        compiler_params=pltpu.CompilerParams(collective_id=0, has_side_effects=True, vmem_limit_bytes=48 * 1024 * 1024),
        cost_estimate=pl.CostEstimate(flops=3_300_000_000, bytes_accessed=6_000_000, transcendentals=0),
    )
    return tuple(call(block_live, key_gate, value_input, filter_taps, cotangent, out_gate, *map(jnp.asarray, consts)))


def solution(mesh):
    spec = P("dp", "ctx", None)
    return jax.shard_map(
        local,
        mesh=mesh,
        in_specs=(spec, spec, spec, P("ctx", None), spec, P("dp", "ctx")),
        out_specs=(spec, spec, spec, P("ctx", None)),
        check_vma=False,
    )
```

time: 642 us -> 91 us (0.14)
  waiting for transfers between devices: 504 us -> 0 us
  Pallas kernels: 0 us -> 75.2 us
  starting transfers between devices: 58 us -> 0 us
  local copies, waits for them, and re-layouts: 35.6 us -> 14.6 us
  matrix products: 20.7 us -> 0 us
  between operations: 14.6 us -> 0.66 us
  other arithmetic: 8.59 us -> 0 us
    all_to_all x8 -> x0, waiting for transfers between devices: 359 us -> none  [the longest x2 141 us: inverse_transform(): lax.all_to_all(twisted, 'ctx', split_axis=3, concat_axis=2, tiled=True)]
    psum x1 -> x0, waiting for transfers between devices: 145 us -> none  [local(): lax.psum(taps_seq.reshape(tok_count, chan_count).astype(jnp.float32).asty...]
    pallas_call x0 -> x1, Pallas kernels: none -> 75.2 us  [local(): call(block_live, key_gate, value_input, filter_taps, cotangent, out_gate,...]
    all_to_all x8 -> x0, starting transfers between devices: 57.7 us -> none  [the longest x2 20.9 us: forward_transform(): lax.all_to_all(signals, 'ctx', split_axis=2, concat_axis=1, tiled=True)]
    dot_general x24 -> x0, matrix products: 20.7 us -> none  [the longest x2 3.5 us: forward_transform(): jnp.einsum('saqc,qk->sakc', imag_in, cos_cols, preferred_element_type=jnp...]
    another operation x9 -> x0, local copies, waits for them, and re-layouts: 14 us -> none  [the longest x2 6.25 us: forward_transform(): packed = jnp.stack([real_part, imag_part]).astype(jnp.bfloat16)]
    unnamed x27 -> x28, local copies, waits for them, and re-layouts: 4.18 us -> 14.6 us
    slice x9 -> x0, local copies, waits for them, and re-layouts: 8.79 us -> none  [the longest x4 6.58 us: forward_transform(): imag_in = regrouped[1]]
  transfers between devices with their start and end apart: 9 -> 0, of which waited for: 9 -> 0; matrix products, arithmetic and copies ran while one was open for 6% -> 0% of each run, Pallas kernels for 0% -> 0%
where the time goes in v1:
time: 91 us; the launch traced here: 90.5 us
  Pallas kernels  75.2 us (83%)
  local copies, waits for them, and re-layouts  14.6 us (16%)
    pallas_call x1, Pallas kernels, local(): call(block_live, key_gate, value_input, filter_taps, cotangent, out_gate,...  75.2 us
    unnamed x28, local copies, waits for them, and re-layouts  14.6 us

profile of v1, /device:TPU:1, one launch (start us, length us, event | category | flops | bytes accessed | tf_op | source)
XLA Modules:
  0.0 90.5 jit_solution(5236964550308579885)
XLA Ops:
  0.6 0.0 copy-start
  0.6 0.9 %copy-done = bf16[1,256,512]{2,1,0:T(8,128)(2,1)S(1)} copy-done((bf16[1,256,512]{2,1,0:T(8,128)(2,1)S(1)}, bf16[1,256,512]{2,1,0:T(8,128)(2,1)}, u32[]{:S(2)}) %copy-start) | copy-done | bytes 262168
  1.6 0.0 copy-start.1
  1.6 0.9 %copy-done.1 = bf16[1,256,512]{2,1,0:T(8,128)(2,1)S(1)} copy-done((bf16[1,256,512]{2,1,0:T(8,128)(2,1)S(1)}, bf16[1,256,512]{2,1,0:T(8,128)(2,1)}, u32[]{:S(2)}) %copy-start.1) | copy-done | bytes 262168
  2.5 0.0 copy-start.2
  2.5 0.9 %copy-done.2 = bf16[256,512]{1,0:T(8,128)(2,1)S(1)} copy-done((bf16[256,512]{1,0:T(8,128)(2,1)S(1)}, bf16[256,512]{1,0:T(8,128)(2,1)}, u32[]{:S(2)}) %copy-start.2) | copy-done | bytes 262168
  3.5 0.0 copy-start.3
  3.5 0.9 %copy-done.3 = bf16[1,256,512]{2,1,0:T(8,128)(2,1)S(1)} copy-done((bf16[1,256,512]{2,1,0:T(8,128)(2,1)S(1)}, bf16[1,256,512]{2,1,0:T(8,128)(2,1)}, u32[]{:S(2)}) %copy-start.3) | copy-done | bytes 262168
  4.4 0.0 copy-start.4
  4.4 0.9 %copy-done.4 = bf16[1,256,512]{2,1,0:T(8,128)(2,1)S(1)} copy-done((bf16[1,256,512]{2,1,0:T(8,128)(2,1)S(1)}, bf16[1,256,512]{2,1,0:T(8,128)(2,1)}, u32[]{:S(2)}) %copy-start.4) | copy-done | bytes 262168
  5.4 0.0 copy-start.5
  5.4 0.7 copy-done.5
  6.0 0.0 copy-start.6
  6.0 1.2 %copy-done.6 = bf16[512,1024]{1,0:T(8,128)(2,1)S(1)} copy-done((bf16[512,1024]{1,0:T(8,128)(2,1)S(1)}, bf16[512,1024]{1,0:T(8,128)(2,1)}, u32[]{:S(2)}) %copy-start.6) | copy-done | bytes 1048600
  7.3 0.0 copy-start.7
  7.3 1.2 %copy-done.7 = bf16[1024,512]{1,0:T(8,128)(2,1)S(1)} copy-done((bf16[1024,512]{1,0:T(8,128)(2,1)S(1)}, bf16[1024,512]{1,0:T(8,128)(2,1)}, u32[]{:S(2)}) %copy-start.7) | copy-done | bytes 1048600
  8.5 0.0 copy-start.8
  8.5 1.0 %copy-done.8 = bf16[512,512]{1,0:T(8,128)(2,1)S(1)} copy-done((bf16[512,512]{1,0:T(8,128)(2,1)S(1)}, bf16[512,512]{1,0:T(8,128)(2,1)}, u32[]{:S(2)}) %copy-start.8) | copy-done | bytes 524312
  9.5 0.0 copy-start.9
  9.5 1.0 %copy-done.9 = bf16[512,512]{1,0:T(8,128)(2,1)S(1)} copy-done((bf16[512,512]{1,0:T(8,128)(2,1)S(1)}, bf16[512,512]{1,0:T(8,128)(2,1)}, u32[]{:S(2)}) %copy-start.9) | copy-done | bytes 524312
  10.6 0.0 copy-start.10
  10.6 1.0 %copy-done.10 = f32[33,8,256]{2,1,0:T(8,128)S(1)} copy-done((f32[33,8,256]{2,1,0:T(8,128)S(1)}, f32[33,8,256]{2,1,0:T(8,128)}, u32[]{:S(2)}) %copy-start.10) | copy-done | bytes 270360
  11.5 0.0 copy-start.11
  11.5 1.0 %copy-done.11 = f32[33,8,256]{2,1,0:T(8,128)S(1)} copy-done((f32[33,8,256]{2,1,0:T(8,128)S(1)}, f32[33,8,256]{2,1,0:T(8,128)}, u32[]{:S(2)}) %copy-start.11) | copy-done | bytes 270360
  12.5 75.2 %shard_map.147 = (bf16[1,256,512]{2,1,0:T(8,128)(2,1)S(1)}, bf16[1,256,512]{2,1,0:T(8,128)(2,1)S(1)}, bf16[1,256,512]{2,1,0:T(8,128)(2,1)S(1)}, bf16[256,512]{1,0:T(8,128)(2,1)S(1)}) custom-call(s32[1,4]{1,0:T(1,128)S(1)} %copy-done.5, bf16[1,256,512]{2,1,0:T(8,128)(2,1)S(1)} %copy-done, bf16[1,256,512]{2,1,0:T(8,128)(2,1)S(1)} %copy-done.1, ...), custom_call_target="tpu_custom_call" | custom-call | flops 3300000000 | bytes 6000000 | tf_op jit(solution)/shard_map/pallas_call | solution.py:404
  87.7 0.7 copy.20
  88.4 0.7 copy.21
  89.1 0.7 copy.22
  89.8 0.7 copy.23
Async XLA Ops:
  0.6 1.0 %copy-start = (bf16[1,256,512]{2,1,0:T(8,128)(2,1)S(1)}, bf16[1,256,512]{2,1,0:T(8,128)(2,1)}, u32[]{:S(2)}) copy-start(bf16[1,256,512]{2,1,0:T(8,128)(2,1)} %key_hbm.1) | copy-start | bytes 786436
  1.6 0.9 %copy-start.1 = (bf16[1,256,512]{2,1,0:T(8,128)(2,1)S(1)}, bf16[1,256,512]{2,1,0:T(8,128)(2,1)}, u32[]{:S(2)}) copy-start(bf16[1,256,512]{2,1,0:T(8,128)(2,1)} %val_hbm.1) | copy-start | bytes 786436
  2.5 0.9 %copy-start.2 = (bf16[256,512]{1,0:T(8,128)(2,1)S(1)}, bf16[256,512]{1,0:T(8,128)(2,1)}, u32[]{:S(2)}) copy-start(bf16[256,512]{1,0:T(8,128)(2,1)} %taps_hbm.1) | copy-start | bytes 786436
  3.5 0.9 %copy-start.3 = (bf16[1,256,512]{2,1,0:T(8,128)(2,1)S(1)}, bf16[1,256,512]{2,1,0:T(8,128)(2,1)}, u32[]{:S(2)}) copy-start(bf16[1,256,512]{2,1,0:T(8,128)(2,1)} %cot_hbm.1) | copy-start | bytes 786436
  4.4 0.9 %copy-start.4 = (bf16[1,256,512]{2,1,0:T(8,128)(2,1)S(1)}, bf16[1,256,512]{2,1,0:T(8,128)(2,1)}, u32[]{:S(2)}) copy-start(bf16[1,256,512]{2,1,0:T(8,128)(2,1)} %gate_hbm.1) | copy-start | bytes 786436
  5.4 0.7 copy-start.5
  6.0 1.2 %copy-start.6 = (bf16[512,1024]{1,0:T(8,128)(2,1)S(1)}, bf16[512,1024]{1,0:T(8,128)(2,1)}, u32[]{:S(2)}) copy-start(bf16[512,1024]{1,0:T(8,128)(2,1)} %constant.15.clone.last_hbm) | copy-start | bytes 3145732
  7.3 1.2 %copy-start.7 = (bf16[1024,512]{1,0:T(8,128)(2,1)S(1)}, bf16[1024,512]{1,0:T(8,128)(2,1)}, u32[]{:S(2)}) copy-start(bf16[1024,512]{1,0:T(8,128)(2,1)} %constant.12.clone.first_hbm) | copy-start | bytes 3145732
  8.5 1.0 %copy-start.8 = (bf16[512,512]{1,0:T(8,128)(2,1)S(1)}, bf16[512,512]{1,0:T(8,128)(2,1)}, u32[]{:S(2)}) copy-start(bf16[512,512]{1,0:T(8,128)(2,1)} %constant.14.clone.inv_hbm) | copy-start | bytes 1572868
  9.5 1.0 %copy-start.9 = (bf16[512,512]{1,0:T(8,128)(2,1)S(1)}, bf16[512,512]{1,0:T(8,128)(2,1)}, u32[]{:S(2)}) copy-start(bf16[512,512]{1,0:T(8,128)(2,1)} %constant.13.clone.fwd_hbm) | copy-start | bytes 1572868
  10.6 1.0 %copy-start.10 = (f32[33,8,256]{2,1,0:T(8,128)S(1)}, f32[33,8,256]{2,1,0:T(8,128)}, u32[]{:S(2)}) copy-start(f32[33,8,256]{2,1,0:T(8,128)} %constant.17.clone.tsin_hbm) | copy-start | bytes 811012
  11.5 1.0 %copy-start.11 = (f32[33,8,256]{2,1,0:T(8,128)S(1)}, f32[33,8,256]{2,1,0:T(8,128)}, u32[]{:S(2)}) copy-start(f32[33,8,256]{2,1,0:T(8,128)} %constant.16.clone.tcos_hbm) | copy-start | bytes 811012

commit v2 on v1

--- a/solution.py
+++ b/solution.py
@@ -53,10 +53,10 @@
     last_hbm,
     tcos_hbm,
     tsin_hbm,
-    out_gate,
-    out_key,
-    out_val,
-    out_taps,
+    gate_out,
+    key_out,
+    val_out,
+    taps_out,
     key,
     val,
     taps,
@@ -86,10 +86,16 @@
     spec_b,
     spec_h,
     twisted,
+    out_gate,
+    out_key,
+    out_val,
+    out_taps,
     load_sem,
     send_sem,
     recv_sem,
     small_sem,
+    block_sem,
+    store_sem,
 ):
     n_dp, n_ctx = devices
     n_z = n_ctx // 2
@@ -99,6 +105,8 @@
     chans, length = n_ctx * gated_s.shape[1], gated_s.shape[2]
     group = gated_s.shape[1]
     n_low = n_ctx + 1
+    n_blocks = max(1, chans // 128)
+    per_block, wide = n_ctx // n_blocks, chans // n_blocks
     blocks = live.shape[1]
     block = length // blocks
 
@@ -152,16 +160,20 @@
     def await_bytes(ref, sem):
         pltpu.make_async_copy(ref, ref, sem).wait()
 
-    def exchange(src, dst, phase):
+    def exchange(src, dst, phase, sem_of=None, start=1, stop=None):
+        recv = recv_sem.at[phase] if sem_of is None else sem_of
+
         def body(k, carry):
-            zz = k // 2
+            far = n_ctx - k
+            zz = far // 2
             away = ((zz + 1) // 2) * (2 * (zz % 2) - 1)
-            to = 2 * ((z + away + n_z) % n_z) + (x + k) % 2
-            remote(src.at[to], dst.at[c], send_sem.at[phase], recv_sem.at[phase], (d, to)).start()
+            to = 2 * ((z + away + n_z) % n_z) + (x + far) % 2
+            remote(src.at[to], dst.at[c], send_sem.at[phase], recv, (d, to)).start()
             return carry
 
-        lax.fori_loop(1, n_ctx, body, 0)
-        dst[c] = src[c]
+        lax.fori_loop(start, n_ctx if stop is None else stop, body, 0)
+        if start == 1:
+            dst[c] = src[c]
 
     def exchanged(dst, phase):
         await_bytes(dst.at[pl.ds(0, n_ctx - 1)], recv_sem.at[phase])
@@ -304,7 +316,8 @@
     sums_r[d] = taps_s[pl.ds(2 * pair_in, 2)]
 
     restore(spec_b, spec_h, True, grad_s, inv_len)
-    exchange(grad_s, grad_r, 5)
+    ahead = 1 + n_ctx // 5
+    exchange(grad_s, grad_r, 5, block_sem.at[c // per_block], 1, ahead)
 
     await_bytes(sums_r.at[pl.ds(0, n_dp - 1)], recv_sem.at[4])
     taps_scale = 1.0 / math.sqrt(n_dp * n_ctx * length)
@@ -328,11 +341,20 @@
     def _():
         taps_r[c] = total[x]
 
-    def tokens(ref):
-        return ref[...].reshape(chans, length).T.astype(F32)
+    exchange(grad_s, grad_r, 5, block_sem.at[c // per_block], ahead)
+
+    def tokens(values):
+        return values.reshape(-1, length).T.astype(F32)
+
+    stores = []
+
+    def store(src, dst):
+        stores.append(pltpu.make_async_copy(src, dst, store_sem.at[len(stores)]))
+        stores[-1].start()
 
     exchanged(conv_r, 3)
-    out_gate[0] = (cot[0].astype(F32) * tokens(conv_r)).astype(BF16)
+    out_gate[0] = (cot[0].astype(F32) * tokens(conv_r[...])).astype(BF16)
+    store(out_gate, gate_out)
 
     taps_other.wait_recv()
 
@@ -343,14 +365,21 @@
     spread_dp(taps_r, 2 * pair_out, 6)
     await_bytes(taps_r.at[pl.ds(0, 2 * (n_dp - 1))], recv_sem.at[6])
     out_taps[...] = taps_r[...].reshape(chans, length).T
-
-    exchanged(grad_r, 5)
-    grad = tokens(grad_r)
-    for b in range(blocks):
-        rows = slice(b * block, (b + 1) * block)
-        alive = live[0, b].astype(F32)
-        out_key[0, rows] = (grad[rows] * val[0, rows].astype(F32) * alive).astype(BF16)
-        out_val[0, rows] = (grad[rows] * key[0, rows].astype(F32) * alive).astype(BF16)
+    store(out_taps, taps_out)
+
+    order = sorted(range(n_blocks), key=lambda r: -min(r, n_blocks - r))
+    for rel in order:
+        at = (c // per_block + rel) % n_blocks
+        await_bytes(grad_r.at[pl.ds(0, per_block - (rel == 0))], block_sem.at[at])
+        grad = tokens(grad_r[pl.ds(at * per_block, per_block)])
+        lanes = pl.ds(pl.multiple_of(at * wide, wide), wide)
+        for b in range(blocks):
+            rows = slice(b * block, (b + 1) * block)
+            alive = live[0, b].astype(F32)
+            out_key[0, rows, lanes] = (grad[rows] * val[0, rows, lanes].astype(F32) * alive).astype(BF16)
+            out_val[0, rows, lanes] = (grad[rows] * key[0, rows, lanes].astype(F32) * alive).astype(BF16)
+        store(out_key.at[:, :, lanes], key_out.at[:, :, lanes])
+        store(out_val.at[:, :, lanes], val_out.at[:, :, lanes])
 
     filt_other.wait_send()
     taps_other.wait_send()
@@ -364,6 +393,23 @@
         exchange_sent(src, phase)
     for ref, phase in ((filt_r, 2), (taps_s, 4), (taps_r, 6)):
         await_bytes(ref.at[pl.ds(0, 2 * (n_dp - 1))], send_sem.at[phase])
+    for copy in stores:
+        copy.wait()
+
+
+def copy_kernel(*refs):
+    count = (len(refs) - 2) // 3
+    sources, targets, stages = refs[:count], refs[count : 2 * count], refs[2 * count : 3 * count]
+    load_sem, store_sem = refs[3 * count :]
+    loads = [pltpu.make_async_copy(sources[i], stages[i], load_sem.at[i]) for i in range(count)]
+    stores = [pltpu.make_async_copy(stages[i], targets[i], store_sem.at[i]) for i in range(count)]
+    for load in loads:
+        load.start()
+    for load, store in zip(loads, stores):
+        load.wait()
+        store.start()
+    for store in stores:
+        store.wait()
 
 
 def local(out_gate, key_gate, value_input, filter_taps, cotangent, block_live):
@@ -371,10 +417,11 @@
     length, chans = key_gate.shape[1:]
     group = chans // n_ctx
     consts = tables(n_ctx, length, group)
-    any_spec = pl.BlockSpec(memory_space=pl.ANY)
+    hbm_spec = pl.BlockSpec(memory_space=pltpu.HBM)
     signal = (1, length, chans)
     chunks = pltpu.VMEM((n_ctx, group, length), BF16)
     rows = (n_ctx + 1) * group
+    n_blocks = max(1, chans // 128)
     scratch = (
         [pltpu.VMEM(signal, BF16)] * 2
         + [pltpu.VMEM(signal[1:], BF16)]
@@ -384,24 +431,37 @@
         + [pltpu.VMEM((n_dp, 2, group, length), BF16), pltpu.VMEM((2, group, length), BF16), chunks]
         + [pltpu.VMEM((rows, 2 * length), F32)] * 3
         + [pltpu.VMEM((2 * n_ctx * group, length), BF16)]
+        + [pltpu.VMEM(signal, BF16)] * 3
+        + [pltpu.VMEM(signal[1:], BF16)]
         + [
             pltpu.SemaphoreType.DMA((11,)),
             pltpu.SemaphoreType.DMA((7,)),
             pltpu.SemaphoreType.DMA((7,)),
             pltpu.SemaphoreType.DMA((4, 2)),
+            pltpu.SemaphoreType.DMA((n_blocks,)),
+            pltpu.SemaphoreType.DMA((2 + 2 * n_blocks,)),
         ]
     )
-    vmem_spec = pl.BlockSpec(memory_space=pltpu.VMEM)
+    out_shape = [jax.ShapeDtypeStruct(signal, BF16)] * 3 + [jax.ShapeDtypeStruct(signal[1:], BF16)]
     call = pl.pallas_call(
         functools.partial(kernel, (n_dp, n_ctx)),
-        out_shape=[jax.ShapeDtypeStruct(signal, BF16)] * 3 + [jax.ShapeDtypeStruct(signal[1:], BF16)],
-        in_specs=[pl.BlockSpec(memory_space=pltpu.SMEM)] + [any_spec] * 11,
-        out_specs=[vmem_spec] * 4,
+        out_shape=out_shape,
+        in_specs=[pl.BlockSpec(memory_space=pltpu.SMEM)] + [hbm_spec] * 11,
+        out_specs=[hbm_spec] * 4,
         scratch_shapes=scratch,
-        compiler_params=pltpu.CompilerParams(collective_id=0, has_side_effects=True, vmem_limit_bytes=48 * 1024 * 1024),
+        compiler_params=pltpu.CompilerParams(collective_id=0, has_side_effects=True, vmem_limit_bytes=60 * 1024 * 1024),
         cost_estimate=pl.CostEstimate(flops=3_300_000_000, bytes_accessed=6_000_000, transcendentals=0),
     )
-    return tuple(call(block_live, key_gate, value_input, filter_taps, cotangent, out_gate, *map(jnp.asarray, consts)))
+    results = call(block_live, key_gate, value_input, filter_taps, cotangent, out_gate, *map(jnp.asarray, consts))
+    final = pl.pallas_call(
+        copy_kernel,
+        out_shape=out_shape,
+        in_specs=[hbm_spec] * 4,
+        out_specs=[hbm_spec] * 4,
+        scratch_shapes=[pltpu.VMEM(o.shape, BF16) for o in out_shape] + [pltpu.SemaphoreType.DMA((4,))] * 2,
+        cost_estimate=pl.CostEstimate(flops=0, bytes_accessed=2_000_000, transcendentals=0),
+    )
+    return tuple(final(*results))
 
 
 def solution(mesh):

time: 91 us -> 72.8 us (0.80)
  local copies, waits for them, and re-layouts: 14.6 us -> 0 us
  Pallas kernels: 75.2 us -> 72 us
    unnamed x28 -> x0, local copies, waits for them, and re-layouts: 14.6 us -> none
    pallas_call x1, Pallas kernels: 75.2 us -> 70 us  [local(): call(block_live, key_gate, value_input, filter_taps, cotangent, out_gate,...]
    pallas_call x0 -> x1, Pallas kernels: none -> 1.98 us  [local(): return tuple(final(*results))]
where the time goes in v2:
time: 72.8 us; the launch traced here: 72.7 us
  Pallas kernels  72 us (99%)
    pallas_call x1, Pallas kernels, local(): call(block_live, key_gate, value_input, filter_taps, cotangent, out_gate,...  70 us
    pallas_call x1, Pallas kernels, local(): return tuple(final(*results))  1.98 us

profile of v2, /device:TPU:1, one launch (start us, length us, event | category | flops | bytes accessed | tf_op | source)
XLA Modules:
  0.0 72.7 jit_solution(15533328196282698049)
XLA Ops:
  0.6 70.0 %shard_map.147 = (bf16[1,256,512]{2,1,0:T(8,128)(2,1)}, bf16[1,256,512]{2,1,0:T(8,128)(2,1)}, bf16[1,256,512]{2,1,0:T(8,128)(2,1)}, bf16[256,512]{1,0:T(8,128)(2,1)}) custom-call(s32[1,4]{1,0:T(1,128)} %live.1, bf16[1,256,512]{2,1,0:T(8,128)(2,1)} %key_hbm.1, bf16[1,256,512]{2,1,0:T(8,128)(2,1)} %val_hbm.1, bf16[256,512]{1,0:T(8,128)(2,1)} %taps_hbm.1, ...), custom_call_target="tpu_custom_call" | custom-call | flops 3300000000 | bytes 6000000 | tf_op jit(solution)/shard_map/pallas_call | solution.py:455
  70.7 2.0 %shard_map.148 = (bf16[1,256,512]{2,1,0:T(8,128)(2,1)}, bf16[1,256,512]{2,1,0:T(8,128)(2,1)}, bf16[1,256,512]{2,1,0:T(8,128)(2,1)}, bf16[256,512]{1,0:T(8,128)(2,1)}) custom-call(bf16[1,256,512]{2,1,0:T(8,128)(2,1)} %get-tuple-element.8.refs_0_, bf16[1,256,512]{2,1,0:T(8,128)(2,1)} %get-tuple-element.9.refs_1_, ...), custom_call_target="tpu_custom_call" | custom-call | bytes 2000000 | tf_op jit(solution)/shard_map/pallas_call | solution.py:464

commit v3 on v2

--- a/solution.py
+++ b/solution.py
@@ -56,7 +56,7 @@
     gate_out,
     key_out,
     val_out,
-    taps_out,
+    shared,
     key,
     val,
     taps,
@@ -89,7 +89,6 @@
     out_gate,
     out_key,
     out_val,
-    out_taps,
     load_sem,
     send_sem,
     recv_sem,
@@ -181,11 +180,11 @@
     def exchange_sent(src, phase):
         await_bytes(src.at[pl.ds(0, n_ctx - 1)], send_sem.at[phase])
 
-    def spread_dp(ref, place, phase):
+    def spread_dp(ref, dst, place, phase):
         def body(k, carry):
             to = (d + k) % n_dp
-            part = ref.at[pl.ds(place, 2)]
-            remote(part, part, send_sem.at[phase], recv_sem.at[phase], (to, c)).start()
+            part = pl.ds(place, 2)
+            remote(ref.at[part], dst.at[part], send_sem.at[phase], recv_sem.at[phase], (to, c)).start()
             return carry
 
         lax.fori_loop(1, n_dp, body, 0)
@@ -233,7 +232,7 @@
     def _():
         filt_same.wait_recv()
 
-    spread_dp(filt_r, 2 * pair_in, 2)
+    spread_dp(filt_r, filt_r, 2 * pair_in, 2)
     for load in loads[5:]:
         load.wait()
 
@@ -362,11 +361,9 @@
     def _():
         taps_same.wait_recv()
 
-    spread_dp(taps_r, 2 * pair_out, 6)
-    await_bytes(taps_r.at[pl.ds(0, 2 * (n_dp - 1))], recv_sem.at[6])
-    out_taps[...] = taps_r[...].reshape(chans, length).T
-    store(out_taps, taps_out)
-
+    mine = pl.ds(2 * pair_out, 2)
+    store(taps_r.at[mine], shared.at[mine])
+    spread_dp(taps_r, shared, 2 * pair_out, 6)
     order = sorted(range(n_blocks), key=lambda r: -min(r, n_blocks - r))
     for rel in order:
         at = (c // per_block + rel) % n_blocks
@@ -381,6 +378,8 @@
         store(out_key.at[:, :, lanes], key_out.at[:, :, lanes])
         store(out_val.at[:, :, lanes], val_out.at[:, :, lanes])
 
+    await_bytes(shared.at[pl.ds(0, 2 * (n_dp - 1))], recv_sem.at[6])
+
     filt_other.wait_send()
     taps_other.wait_send()
 
@@ -397,15 +396,17 @@
         copy.wait()
 
 
-def copy_kernel(*refs):
-    count = (len(refs) - 2) // 3
-    sources, targets, stages = refs[:count], refs[count : 2 * count], refs[2 * count : 3 * count]
-    load_sem, store_sem = refs[3 * count :]
-    loads = [pltpu.make_async_copy(sources[i], stages[i], load_sem.at[i]) for i in range(count)]
-    stores = [pltpu.make_async_copy(stages[i], targets[i], store_sem.at[i]) for i in range(count)]
+def finish(gate, key, val, shared, gate_out, key_out, val_out, taps_out, gate_v, key_v, val_v, shared_v, taps_v, load_sem, store_sem):
+    pairs = [(shared, shared_v), (gate, gate_v), (key, key_v), (val, val_v)]
+    loads = [pltpu.make_async_copy(src, dst, load_sem.at[i]) for i, (src, dst) in enumerate(pairs)]
+    pairs = [(taps_v, taps_out), (gate_v, gate_out), (key_v, key_out), (val_v, val_out)]
+    stores = [pltpu.make_async_copy(src, dst, store_sem.at[i]) for i, (src, dst) in enumerate(pairs)]
     for load in loads:
         load.start()
-    for load, store in zip(loads, stores):
+    loads[0].wait()
+    taps_v[...] = shared_v[...].reshape(-1, shared_v.shape[2]).T
+    stores[0].start()
+    for load, store in zip(loads[1:], stores[1:]):
         load.wait()
         store.start()
     for store in stores:
@@ -432,7 +433,6 @@
         + [pltpu.VMEM((rows, 2 * length), F32)] * 3
         + [pltpu.VMEM((2 * n_ctx * group, length), BF16)]
         + [pltpu.VMEM(signal, BF16)] * 3
-        + [pltpu.VMEM(signal[1:], BF16)]
         + [
             pltpu.SemaphoreType.DMA((11,)),
             pltpu.SemaphoreType.DMA((7,)),
@@ -445,7 +445,7 @@
     out_shape = [jax.ShapeDtypeStruct(signal, BF16)] * 3 + [jax.ShapeDtypeStruct(signal[1:], BF16)]
     call = pl.pallas_call(
         functools.partial(kernel, (n_dp, n_ctx)),
-        out_shape=out_shape,
+        out_shape=out_shape[:3] + [jax.ShapeDtypeStruct(chunks.shape, BF16)],
         in_specs=[pl.BlockSpec(memory_space=pltpu.SMEM)] + [hbm_spec] * 11,
         out_specs=[hbm_spec] * 4,
         scratch_shapes=scratch,
@@ -454,11 +454,13 @@
     )
     results = call(block_live, key_gate, value_input, filter_taps, cotangent, out_gate, *map(jnp.asarray, consts))
     final = pl.pallas_call(
-        copy_kernel,
+        finish,
         out_shape=out_shape,
         in_specs=[hbm_spec] * 4,
         out_specs=[hbm_spec] * 4,
-        scratch_shapes=[pltpu.VMEM(o.shape, BF16) for o in out_shape] + [pltpu.SemaphoreType.DMA((4,))] * 2,
+        scratch_shapes=[pltpu.VMEM(signal, BF16)] * 3
+        + [chunks, pltpu.VMEM(signal[1:], BF16)]
+        + [pltpu.SemaphoreType.DMA((4,))] * 2,
         cost_estimate=pl.CostEstimate(flops=0, bytes_accessed=2_000_000, transcendentals=0),
     )
     return tuple(final(*results))

time: 72.8 us -> 71.9 us (0.988)
  Pallas kernels: 72 us -> 71.1 us
    pallas_call x1, Pallas kernels: 70 us -> 69 us  [local(): call(block_live, key_gate, value_input, filter_taps, cotangent, out_gate,...]
where the time goes in v3:
time: 71.9 us; the launch traced here: 71.8 us
  Pallas kernels  71.1 us (99%)
    pallas_call x1, Pallas kernels, local(): call(block_live, key_gate, value_input, filter_taps, cotangent, out_gate,...  69 us
    pallas_call x1, Pallas kernels, local(): return tuple(final(*results))  2.1 us

profile of v3, /device:TPU:1, one launch (start us, length us, event | category | flops | bytes accessed | tf_op | source)
XLA Modules:
  0.0 71.8 jit_solution(11243864773258957836)
XLA Ops:
  0.6 69.0 %shard_map.147 = (bf16[1,256,512]{2,1,0:T(8,128)(2,1)}, bf16[1,256,512]{2,1,0:T(8,128)(2,1)}, bf16[1,256,512]{2,1,0:T(8,128)(2,1)}, bf16[32,16,256]{2,1,0:T(8,128)(2,1)}) custom-call(s32[1,4]{1,0:T(1,128)} %live.1, bf16[1,256,512]{2,1,0:T(8,128)(2,1)} %key_hbm.1, bf16[1,256,512]{2,1,0:T(8,128)(2,1)} %val_hbm.1, bf16[256,512]{1,0:T(8,128)(2,1)} %taps_hbm.1, ...), custom_call_target="tpu_custom_call" | custom-call | flops 3300000000 | bytes 6000000 | tf_op jit(solution)/shard_map/pallas_call | solution.py:455
  69.7 2.1 %shard_map.148 = (bf16[1,256,512]{2,1,0:T(8,128)(2,1)}, bf16[1,256,512]{2,1,0:T(8,128)(2,1)}, bf16[1,256,512]{2,1,0:T(8,128)(2,1)}, bf16[256,512]{1,0:T(8,128)(2,1)}) custom-call(bf16[1,256,512]{2,1,0:T(8,128)(2,1)} %get-tuple-element.8.gate, bf16[1,256,512]{2,1,0:T(8,128)(2,1)} %get-tuple-element.9.key, bf16[1,256,512]{2,1,0:T(8,128)(2,1)} %get-tuple-element.10.val, ...), custom_call_target="tpu_custom_call" | custom-call | bytes 2000000 | tf_op jit(solution)/shard_map/pallas_call | solution.py:466

commit v4 on v3

--- a/solution.py
+++ b/solution.py
@@ -351,19 +351,19 @@
         stores.append(pltpu.make_async_copy(src, dst, store_sem.at[len(stores)]))
         stores[-1].start()
 
+    taps_other.wait_recv()
+
+    @pl.when(shift != 0)
+    def _():
+        taps_same.wait_recv()
+
+    mine = pl.ds(2 * pair_out, 2)
+    store(taps_r.at[mine], shared.at[mine])
+    spread_dp(taps_r, shared, 2 * pair_out, 6)
+
     exchanged(conv_r, 3)
     out_gate[0] = (cot[0].astype(F32) * tokens(conv_r[...])).astype(BF16)
     store(out_gate, gate_out)
-
-    taps_other.wait_recv()
-
-    @pl.when(shift != 0)
-    def _():
-        taps_same.wait_recv()
-
-    mine = pl.ds(2 * pair_out, 2)
-    store(taps_r.at[mine], shared.at[mine])
-    spread_dp(taps_r, shared, 2 * pair_out, 6)
     order = sorted(range(n_blocks), key=lambda r: -min(r, n_blocks - r))
     for rel in order:
         at = (c // per_block + rel) % n_blocks

time: 71.9 us -> 71.9 us (level)
  no operation moved by 1% of the time
where the time goes in v4:
time: 71.9 us; the launch traced here: 71.8 us
  Pallas kernels  71.1 us (99%)
    pallas_call x1, Pallas kernels, local(): call(block_live, key_gate, value_input, filter_taps, cotangent, out_gate,...  69 us
    pallas_call x1, Pallas kernels, local(): return tuple(final(*results))  2.1 us

profile of v4, /device:TPU:1, one launch (start us, length us, event | category | flops | bytes accessed | tf_op | source)
XLA Modules:
  0.0 71.8 jit_solution(16705286536833645904)
XLA Ops:
  0.6 69.0 %shard_map.147 = (bf16[1,256,512]{2,1,0:T(8,128)(2,1)}, bf16[1,256,512]{2,1,0:T(8,128)(2,1)}, bf16[1,256,512]{2,1,0:T(8,128)(2,1)}, bf16[32,16,256]{2,1,0:T(8,128)(2,1)}) custom-call(s32[1,4]{1,0:T(1,128)} %live.1, bf16[1,256,512]{2,1,0:T(8,128)(2,1)} %key_hbm.1, bf16[1,256,512]{2,1,0:T(8,128)(2,1)} %val_hbm.1, bf16[256,512]{1,0:T(8,128)(2,1)} %taps_hbm.1, ...), custom_call_target="tpu_custom_call" | custom-call | flops 3300000000 | bytes 6000000 | tf_op jit(solution)/shard_map/pallas_call | solution.py:455
  69.7 2.1 %shard_map.148 = (bf16[1,256,512]{2,1,0:T(8,128)(2,1)}, bf16[1,256,512]{2,1,0:T(8,128)(2,1)}, bf16[1,256,512]{2,1,0:T(8,128)(2,1)}, bf16[256,512]{1,0:T(8,128)(2,1)}) custom-call(bf16[1,256,512]{2,1,0:T(8,128)(2,1)} %get-tuple-element.8.gate, bf16[1,256,512]{2,1,0:T(8,128)(2,1)} %get-tuple-element.9.key, bf16[1,256,512]{2,1,0:T(8,128)(2,1)} %get-tuple-element.10.val, ...), custom_call_target="tpu_custom_call" | custom-call | bytes 2000000 | tf_op jit(solution)/shard_map/pallas_call | solution.py:466
